TPU v7x, 32 devices: a whole 2x2x4 slice. The times are simulated.
32 devices in a mesh: shard: 8 (over y, x, core), tensor: 4 (over z).
Axes of the slice: x: 2, y: 2, z: 4, core: 2. Of those that a mesh axis runs over, the one named last changes fastest.
Arguments:
- tokens: bfloat16 [3072, 1024], P(('shard', 'tensor')), may hold values from -6 to 6
- doc_starts: int32 [2], replicated, may hold values from 0 to 3071, as said below
- norm1_gain: float32 [1024], replicated, may hold values from 0.25 to 1.75
- qkv_weight: bfloat16 [1024, 3, 1024], P('shard', None, 'tensor'), may hold values from -0.25 to 0.25
- out_weight: bfloat16 [1024, 1024], P('shard', 'tensor'), may hold values from -1.25 to 1.25
- norm2_gain: float32 [1024], replicated, may hold values from 0.25 to 1.75
- in_weight: bfloat16 [1024, 2, 2624], P('shard', None, 'tensor'), may hold values from -0.1875 to 0.1875
- down_weight: bfloat16 [1024, 2624], P('shard', 'tensor'), may hold values from -0.25 to 0.25
- cotangent: bfloat16 [3072, 1024], P(('shard', 'tensor')), may hold values from -8 to 8
Outputs:
- mixed: bfloat16 [3072, 1024], P(('shard', 'tensor'))
- tokens_grad: bfloat16 [3072, 1024], P(('shard', 'tensor'))
- norm1_gain_grad: float32 [1024], replicated
- qkv_weight_grad: float32 [1024, 3, 1024], P('shard', None, 'tensor')
- out_weight_grad: float32 [1024, 1024], P('shard', 'tensor')
- norm2_gain_grad: float32 [1024], replicated
- in_weight_grad: float32 [1024, 2, 2624], P('shard', None, 'tensor')
- down_weight_grad: float32 [1024, 2624], P('shard', 'tensor')
Inputs may be any that keep to these rules, and one draw needn't show every extreme that they name: doc_starts rises strictly from 0; the second document begins within the last 192 tokens; no document is longer than 3072 tokens.
All inputs are finite; a program needn't handle non-finite values.
Results may differ from a plain program's by a relative error of at most 0.04.
Values may be sent and summed in bfloat16 or wider, within the bound.
A program may use at most 192 MiB of HBM per device.

v0:
```python
import jax
import jax.numpy as jnp
from jax import lax
from jax.sharding import PartitionSpec as P

HEAD_DIM = 64


EPSILON = 1e-05
THETA = 160000.0
MASKED = -1e30


def norm_rows(values, gain):
    centred = values - jnp.mean(values, axis=-1, keepdims=True)
    variance = jnp.mean(centred * centred, axis=-1, keepdims=True)
    return centred * lax.rsqrt(variance + EPSILON) * gain


def doc_layout(index, doc_starts):
    begun = doc_starts[None, :] <= index[:, None]
    segment = jnp.sum(begun.astype(jnp.int32), axis=1) - 1
    opening = jnp.max(jnp.where(begun, doc_starts[None, :], 0), axis=1)
    return (segment, index - opening)


def turning(position, head_width):
    halfway = head_width // 2
    inverse = THETA ** (-jnp.arange(halfway, dtype=jnp.float32) * 2.0 / head_width)
    angles = position.astype(jnp.float32)[:, None] * inverse[None, :]
    return (jnp.cos(angles)[:, None, :], jnp.sin(angles)[:, None, :])


def rotate(values, cosine, sine, direction):
    halfway = values.shape[-1] // 2
    leading = values[..., :halfway]
    trailing = values[..., halfway:]
    return jnp.concatenate(
        [
            leading * cosine - direction * trailing * sine,
            trailing * cosine + direction * leading * sine,
        ],
        axis=-1,
    )


def block_split(row_total):
    for candidate in range(min(row_total, 1536), 0, -1):
        if row_total % candidate == 0:
            return candidate
    return row_total


def geglu(gate, upward):
    return jax.nn.gelu(gate, approximate=False) * upward


def head_scores(query, keys_flat, query_segment, key_segment):
    key_rows = keys_flat.shape[0]
    keys = keys_flat.reshape(key_rows, query.shape[1], query.shape[2])
    scores = jnp.einsum(
        "qhe,khe->hqk", query, keys, preferred_element_type=jnp.float32
    ) * query.shape[2] ** (-0.5)
    shared = query_segment[:, None] == key_segment[None, :]
    return (scores, shared, keys)


def score_grads(
    query, grad_heads, log_total, delta, query_segment, keys_flat, values_flat, key_segment
):
    scores, shared, keys = head_scores(query, keys_flat, query_segment, key_segment)
    values = values_flat.reshape(keys.shape)
    weights = jnp.where(shared[None], jnp.exp(scores - log_total[..., None]), 0.0)
    weight_grad = jnp.einsum("qhe,khe->hqk", grad_heads, values, preferred_element_type=jnp.float32)
    score_grad = (weights * (weight_grad - delta[..., None])).astype(jnp.bfloat16)
    return (weights.astype(jnp.bfloat16), score_grad, keys)


def on_device(
    tokens,
    doc_starts,
    norm1_gain,
    qkv_weight,
    out_weight,
    norm2_gain,
    in_weight,
    down_weight,
    cotangent,
):
    row_count = tokens.shape[0]
    model_width = tokens.shape[1]
    local_width = qkv_weight.shape[2]
    unit_width = in_weight.shape[2]
    head_dim = HEAD_DIM
    heads_here = local_width // head_dim
    group_rows = row_count * lax.axis_size("tensor")
    group_index = lax.axis_index("shard") * group_rows + jnp.arange(group_rows, dtype=jnp.int32)
    segment, position = doc_layout(group_index, doc_starts)
    cosine, sine = turning(position, head_dim)
    contract_rows = (((0,), (0,)), ((), ()))
    contract_cols = (((1,), (1,)), ((), ()))
    shape_heads = (group_rows, heads_here, head_dim)
    qkv_full, out_full, in_full, down_full = (
        lax.all_gather(qkv_weight, "shard", axis=0, tiled=True),
        lax.all_gather(out_weight, "shard", axis=0, tiled=True),
        lax.all_gather(in_weight, "shard", axis=0, tiled=True),
        lax.all_gather(down_weight, "shard", axis=0, tiled=True),
    )
    qkv_mat = qkv_full.reshape(model_width, 3 * local_width)
    in_mat = in_full.reshape(model_width, 2 * unit_width)
    resid_in = tokens.astype(jnp.float32)
    normed_one, norm_one_back = jax.vjp(norm_rows, resid_in, norm1_gain)
    rows_one = lax.all_gather(normed_one.astype(jnp.bfloat16), "tensor", axis=0, tiled=True)
    projected = jnp.dot(rows_one, qkv_mat, preferred_element_type=jnp.float32)
    query = rotate(projected[:, :local_width].reshape(shape_heads), cosine, sine, 1.0).astype(
        jnp.bfloat16
    )
    keys_flat = (
        rotate(projected[:, local_width : 2 * local_width].reshape(shape_heads), cosine, sine, 1.0)
        .astype(jnp.bfloat16)
        .reshape(group_rows, local_width)
    )
    values_flat = projected[:, 2 * local_width :].astype(jnp.bfloat16)
    all_keys, all_values = (
        lax.all_gather(keys_flat, "shard", axis=0, tiled=True),
        lax.all_gather(values_flat, "shard", axis=0, tiled=True),
    )
    all_rows = all_keys.shape[0]
    key_segment, _ = doc_layout(jnp.arange(all_rows, dtype=jnp.int32), doc_starts)
    key_block = block_split(all_rows)
    block_count = all_rows // key_block
    key_stack = (
        all_keys.reshape(block_count, key_block, local_width),
        all_values.reshape(block_count, key_block, local_width),
        key_segment.reshape(block_count, key_block),
    )

    def total_pass(running, entries):
        highest, summed = running
        key_piece, _, segment_piece = entries
        scores, shared, _ = head_scores(query, key_piece, segment, segment_piece)
        masked = jnp.where(shared[None], scores, MASKED)
        raised = jnp.maximum(highest, jnp.max(masked, axis=2))
        fresh = jnp.where(shared[None], jnp.exp(masked - raised[..., None]), 0.0)
        summed = summed * jnp.exp(highest - raised) + jnp.sum(fresh, axis=2)
        return ((raised, summed), None)

    start_totals = (
        jnp.full((heads_here, group_rows), MASKED, jnp.float32),
        jnp.zeros((heads_here, group_rows), jnp.float32),
    )
    (highest, summed), _ = lax.scan(total_pass, start_totals, key_stack)
    log_total = highest + jnp.log(summed)

    def output_pass(running, entries):
        key_piece, value_piece, segment_piece = entries
        scores, shared, _ = head_scores(query, key_piece, segment, segment_piece)
        weights = jnp.where(shared[None], jnp.exp(scores - log_total[..., None]), 0.0).astype(
            jnp.bfloat16
        )
        values = value_piece.reshape(value_piece.shape[0], heads_here, head_dim)
        return (
            running
            + jnp.einsum("hqk,khe->qhe", weights, values, preferred_element_type=jnp.float32),
            None,
        )

    zeros_heads = jnp.zeros(shape_heads, jnp.float32)
    attended_raw, _ = lax.scan(output_pass, zeros_heads, key_stack)
    attended = attended_raw.reshape(group_rows, local_width).astype(jnp.bfloat16)
    piece = attended
    resid_mid = resid_in + lax.psum_scatter(
        lax.dot_general(piece, out_full, contract_cols, preferred_element_type=jnp.float32).astype(
            jnp.bfloat16
        ),
        "tensor",
        scatter_dimension=0,
        tiled=True,
    ).astype(jnp.float32)
    normed_two, norm_two_back = jax.vjp(norm_rows, resid_mid, norm2_gain)
    rows_two = lax.all_gather(normed_two.astype(jnp.bfloat16), "tensor", axis=0, tiled=True)
    gate_up = jnp.dot(rows_two, in_mat, preferred_element_type=jnp.float32)
    active, geglu_back = jax.vjp(geglu, gate_up[:, :unit_width], gate_up[:, unit_width:])
    active = active.astype(jnp.bfloat16)
    piece = active
    mixed = (
        resid_mid
        + lax.psum_scatter(
            lax.dot_general(
                piece, down_full, contract_cols, preferred_element_type=jnp.float32
            ).astype(jnp.bfloat16),
            "tensor",
            scatter_dimension=0,
            tiled=True,
        ).astype(jnp.float32)
    ).astype(jnp.bfloat16)
    cot_full = lax.all_gather(cotangent, "tensor", axis=0, tiled=True)
    down_grad = lax.dot_general(cot_full, active, contract_rows, preferred_element_type=jnp.float32)
    active_grad = jnp.dot(cot_full, down_full, preferred_element_type=jnp.float32)
    gate_grad, up_grad = geglu_back(active_grad)
    gate_up_grad = jnp.concatenate([gate_grad, up_grad], axis=1).astype(jnp.bfloat16)
    in_grad = lax.dot_general(
        rows_two, gate_up_grad, contract_rows, preferred_element_type=jnp.float32
    ).reshape(model_width, 2, unit_width)
    piece = gate_up_grad
    normed_two_grad = lax.psum_scatter(
        lax.dot_general(piece, in_mat, contract_cols, preferred_element_type=jnp.float32).astype(
            jnp.bfloat16
        ),
        "tensor",
        scatter_dimension=0,
        tiled=True,
    ).astype(jnp.float32)
    mid_part, gain_two_grad = norm_two_back(normed_two_grad)
    mid_grad = cotangent.astype(jnp.float32) + mid_part
    branch_full = lax.all_gather(mid_grad.astype(jnp.bfloat16), "tensor", axis=0, tiled=True)
    out_grad = lax.dot_general(
        branch_full, attended, contract_rows, preferred_element_type=jnp.float32
    )
    attended_grad = jnp.dot(branch_full, out_full, preferred_element_type=jnp.float32).astype(
        jnp.bfloat16
    )
    grad_heads = attended_grad.reshape(shape_heads)
    delta = jnp.sum(grad_heads.astype(jnp.float32) * attended_raw, axis=2).T

    def joint_pass(running, entries):
        key_piece, value_piece, segment_piece = entries
        weights, score_grad, keys = score_grads(
            query, grad_heads, log_total, delta, segment, key_piece, value_piece, segment_piece
        )
        running = running + jnp.einsum(
            "hqk,khe->qhe", score_grad, keys, preferred_element_type=jnp.float32
        )
        key_part = jnp.einsum("hqk,qhe->khe", score_grad, query, preferred_element_type=jnp.float32)
        value_part = jnp.einsum(
            "hqk,qhe->khe", weights, grad_heads, preferred_element_type=jnp.float32
        )
        return (running, (key_part, value_part))

    query_rot_grad, (key_parts, value_parts) = lax.scan(joint_pass, zeros_heads, key_stack)
    key_rot_grad, value_grad = (
        lax.psum_scatter(
            key_parts.reshape(all_rows, local_width), "shard", scatter_dimension=0, tiled=True
        ),
        lax.psum_scatter(
            value_parts.reshape(all_rows, local_width), "shard", scatter_dimension=0, tiled=True
        ),
    )
    score_scale = head_dim ** (-0.5)
    query_grad = rotate(query_rot_grad * score_scale, cosine, sine, -1.0).astype(jnp.bfloat16)
    key_grad = rotate(key_rot_grad.reshape(shape_heads) * score_scale, cosine, sine, -1.0).astype(
        jnp.bfloat16
    )
    qkv_grad = jnp.concatenate(
        [
            query_grad.reshape(group_rows, local_width),
            key_grad.reshape(group_rows, local_width),
            value_grad.astype(jnp.bfloat16),
        ],
        axis=1,
    )
    qkv_grad_w = lax.dot_general(
        rows_one, qkv_grad, contract_rows, preferred_element_type=jnp.float32
    ).reshape(model_width, 3, local_width)
    piece = qkv_grad
    normed_one_grad = lax.psum_scatter(
        lax.dot_general(piece, qkv_mat, contract_cols, preferred_element_type=jnp.float32).astype(
            jnp.bfloat16
        ),
        "tensor",
        scatter_dimension=0,
        tiled=True,
    ).astype(jnp.float32)
    input_part, gain_one_grad = norm_one_back(normed_one_grad)
    tokens_grad = (mid_grad + input_part).astype(jnp.bfloat16)
    qkv_piece, out_piece, in_piece, down_piece = (
        lax.psum_scatter(qkv_grad_w, "shard", scatter_dimension=0, tiled=True),
        lax.psum_scatter(out_grad, "shard", scatter_dimension=0, tiled=True),
        lax.psum_scatter(in_grad, "shard", scatter_dimension=0, tiled=True),
        lax.psum_scatter(down_grad, "shard", scatter_dimension=0, tiled=True),
    )
    gain_one_all, gain_two_all = lax.psum((gain_one_grad, gain_two_grad), ("shard", "tensor"))
    return (
        mixed,
        tokens_grad,
        gain_one_all,
        qkv_piece,
        out_piece,
        gain_two_all,
        in_piece,
        down_piece,
    )


def solution(mesh):
    in_specs = (
        P(("shard", "tensor"), None),
        P(),
        P(),
        P("shard", None, "tensor"),
        P("shard", "tensor"),
        P(),
        P("shard", None, "tensor"),
        P("shard", "tensor"),
        P(("shard", "tensor"), None),
    )
    out_specs = (
        P(("shard", "tensor"), None),
        P(("shard", "tensor"), None),
        P(),
        P("shard", None, "tensor"),
        P("shard", "tensor"),
        P(),
        P("shard", None, "tensor"),
        P("shard", "tensor"),
    )
    return jax.shard_map(
        on_device, mesh=mesh, in_specs=in_specs, out_specs=out_specs, check_vma=False
    )
```

profile of v0, /device:TPU:0, one launch (start us, length us, event | category | flops | bytes accessed | tf_op | source)
XLA Modules:
  0.0 768.8 jit_solution(7940525761500336598)
XLA Ops:
  13.0 21.3 %all_gather.30 = bf16[384,1024]{1,0:T(8,128)(2,1)S(1)} all-gather(bf16[96,1024]{1,0:T(8,128)(2,1)S(1)} %fusion.35), channel_id=1, replica_groups=mesh['shard'=8,'tensor'=4] {'tensor'}, dimensions={0}, use_global_device_ids=true | all-gather | bytes 983040 | tf_op jit(solution)/shard_map/all_gather | solution.py:113
  44.8 11.6 %all_gather.34 = bf16[1024,256]{1,0:T(8,128)(2,1)S(1)} all-gather(bf16[128,256]{1,0:T(8,128)(2,1)} %param.19), channel_id=1, replica_groups=mesh['shard'=8,'tensor'=4] {'shard'}, dimensions={0}, use_global_device_ids=true | all-gather | bytes 589824 | tf_op jit(solution)/shard_map/all_gather | solution.py:105
  56.4 12.6 %all-gather.8.cloned.1.call-done = bf16[3072,256]{1,0:T(8,128)(2,1)} async-done(((bf16[384,256]{1,0:T(8,128)(2,1)}), bf16[3072,256]{1,0:T(8,128)(2,1)}) %all-gather.8.cloned.1.call-update) | async-done | bytes 1572880 | tf_op jit(solution)/shard_map/all_gather | solution.py:126
  71.6 25.6 %all-gather.10.cloned.1.call-done = bf16[3072,256]{1,0:T(8,128)(2,1)} async-done(((bf16[384,256]{1,0:T(8,128)(2,1)}), bf16[3072,256]{1,0:T(8,128)(2,1)}) %all-gather.10.cloned.1.call-update) | async-done | bytes 1572880 | tf_op jit(solution)/shard_map/all_gather | solution.py:125
  99.8 11.5 %while.39 = (s32[]{:T(128)}, f32[4,384]{1,0:T(4,128)S(1)}, f32[4,384]{1,0:T(4,128)S(1)}, s32[384]{0:T(512)S(1)}, s32[2,1536]{1,0:T(2,128)S(1)}, /*index=5*/bf16[...) while((s32[]{:T(128)}, f32[4,384]{1,0:T(4,128)S(1)}, ...), condition=%wide.region_8.9_spmd.clone, body=%wide.region_5.8_spmd.clone.sunk | while | flops 321461760 | bytes 23299704 | solution.py:152
  123.3 29.6 %all_gather.38 = bf16[384,1024]{1,0:T(8,128)(2,1)S(1)} all-gather(bf16[96,1024]{1,0:T(8,128)(2,1)S(1)} %copy-done.17), channel_id=1, replica_groups=mesh['shard'=8,'tensor'=4] {'tensor'}, dimensions={0}, use_global_device_ids=true | all-gather | bytes 983040 | tf_op jit(solution)/shard_map/all_gather | solution.py:197
  157.8 20.1 %all_gather.35 = bf16[384,1024]{1,0:T(8,128)(2,1)S(1)} all-gather(bf16[96,1024]{1,0:T(8,128)(2,1)S(1)} %multiply_convert_fusion.2), channel_id=1, replica_groups=mesh['shard'=8,'tensor'=4] {'tensor'}, dimensions={0}, use_global_device_ids=true | all-gather | bytes 983040 | tf_op jit(solution)/shard_map/all_gather | solution.py:181
  177.9 9.9 %all-gather.12.cloned.1.call-done = bf16[1024,2,656]{0,2,1:T(8,128)(2,1)} async-done(((bf16[128,2,656]{0,2,1:T(8,128)(2,1)}), bf16[1024,2,656]{0,2,1:T(8,128)(2,1)}) %all-gather.12.cloned.1.call-update) | async-done | bytes 2686992 | tf_op jit(solution)/shard_map/all_gather | solution.py:106
  192.4 22.0 %all-gather.14.cloned.1.call-done = bf16[1024,656]{0,1:T(8,128)(2,1)} async-done(((bf16[128,656]{0,1:T(8,128)(2,1)}), bf16[1024,656]{0,1:T(8,128)(2,1)}) %all-gather.14.cloned.1.call-update) | async-done | bytes 1343504 | tf_op jit(solution)/shard_map/all_gather | solution.py:107
  227.3 20.3 %reduce-scatter.15.cloned.1.call-done = bf16[96,1024]{1,0:T(8,128)(2,1)} async-done(((bf16[384,1024]{1,0:T(8,128)(2,1)}), bf16[96,1024]{1,0:T(8,128)(2,1)}) %reduce-scatter.15.cloned.1.call-update) | async-done | bytes 196624 | tf_op jit(solution)/shard_map/reduce_scatter | solution.py:206
  249.3 23.1 %reduce-scatter.13.cloned.1.call-done = bf16[96,1024]{1,0:T(8,128)(2,1)} async-done(((bf16[384,1024]{1,0:T(8,128)(2,1)}), bf16[96,1024]{1,0:T(8,128)(2,1)}) %reduce-scatter.13.cloned.1.call-update) | async-done | bytes 196624 | tf_op jit(solution)/shard_map/reduce_scatter | solution.py:188
  275.0 18.0 %all_gather.39 = bf16[384,1024]{1,0:T(8,128)(2,1)S(1)} all-gather(bf16[96,1024]{1,0:T(8,128)(2,1)S(1)} %fusion.44), channel_id=1, replica_groups=mesh['shard'=8,'tensor'=4] {'tensor'}, dimensions={0}, use_global_device_ids=true | all-gather | bytes 983040 | tf_op jit(solution)/shard_map/all_gather | solution.py:216
  295.0 140.4 %while.41 = (s32[]{:T(128)}, f32[384,4,64]{0,2,1:T(8,128)}, f32[2,1536,4,64]{1,0,3,2:T(2,128)}, f32[2,1536,4,64]{1,0,3,2:T(2,128)}, bf16[2,1536,256]{1,2,0:T(8,1...) while((s32[]{:T(128)}, f32[384,4,64]{0,2,1:T(8,128)}, ...), condition=%wide.region_20.21_spmd.clone, body=%wide.region_19.20_spmd.clone.sunk | while | flops 1534328832 | bytes 67180320 | solution.py:240
  312.7 26.0 %dynamic_update_slice.12 = f32[2,1536,4,64]{1,0,3,2:T(2,128)} dynamic-update-slice(f32[2,1536,4,64]{1,0,3,2:T(2,128)} %get-tuple-element.670, f32[1,1536,4,64]{1,0,3,2:T(1,128)S(1)} %copy.85, s32[]{:T(128)S(6)} %copy.107, s32[]{:T(128)} %constant.39.clone.1..sunk.2, s32[]{:T(128)} %constant.39.clone.1..sunk.2, s32[]{:T(128)} %constant.39.clone.1..sunk.2) | dynamic-update-slice | bytes 3145732 | tf_op jit(solution)/shard_map/while/body/jit(dynamic_update_index_in_dim)/dynamic_update_slice | solution.py:240
  338.7 26.1 %dynamic_update_slice.11 = f32[2,1536,4,64]{1,0,3,2:T(2,128)} dynamic-update-slice(f32[2,1536,4,64]{1,0,3,2:T(2,128)} %get-tuple-element.669, f32[1,1536,4,64]{1,0,3,2:T(1,128)S(1)} %copy.84, s32[]{:T(128)S(6)} %copy.107, s32[]{:T(128)} %constant.39.clone.1..sunk.2, s32[]{:T(128)} %constant.39.clone.1..sunk.2, s32[]{:T(128)} %constant.39.clone.1..sunk.2) | dynamic-update-slice | bytes 3145732 | tf_op jit(solution)/shard_map/while/body/jit(dynamic_update_index_in_dim)/dynamic_update_slice | solution.py:240
  383.2 26.0 %dynamic_update_slice.12 = f32[2,1536,4,64]{1,0,3,2:T(2,128)} dynamic-update-slice(f32[2,1536,4,64]{1,0,3,2:T(2,128)} %get-tuple-element.670, f32[1,1536,4,64]{1,0,3,2:T(1,128)S(1)} %copy.85, s32[]{:T(128)S(6)} %copy.107, s32[]{:T(128)} %constant.39.clone.1..sunk.2, s32[]{:T(128)} %constant.39.clone.1..sunk.2, s32[]{:T(128)} %constant.39.clone.1..sunk.2) | dynamic-update-slice | bytes 3145732 | tf_op jit(solution)/shard_map/while/body/jit(dynamic_update_index_in_dim)/dynamic_update_slice | solution.py:240
  409.3 26.1 %dynamic_update_slice.11 = f32[2,1536,4,64]{1,0,3,2:T(2,128)} dynamic-update-slice(f32[2,1536,4,64]{1,0,3,2:T(2,128)} %get-tuple-element.669, f32[1,1536,4,64]{1,0,3,2:T(1,128)S(1)} %copy.84, s32[]{:T(128)S(6)} %copy.107, s32[]{:T(128)} %constant.39.clone.1..sunk.2, s32[]{:T(128)} %constant.39.clone.1..sunk.2, s32[]{:T(128)} %constant.39.clone.1..sunk.2) | dynamic-update-slice | bytes 3145732 | tf_op jit(solution)/shard_map/while/body/jit(dynamic_update_index_in_dim)/dynamic_update_slice | solution.py:240
  444.8 40.4 %reduce-scatter.17.cloned.1.call-done = f32[384,256]{0,1:T(8,128)} async-done(((f32[3072,256]{0,1:T(8,128)}), f32[384,256]{0,1:T(8,128)}) %reduce-scatter.17.cloned.1.call-update) | async-done | bytes 393232 | tf_op jit(solution)/shard_map/reduce_scatter | solution.py:242
  486.5 48.6 %reduce-scatter.19.cloned.1.call-done = f32[384,256]{0,1:T(8,128)} async-done(((f32[3072,256]{0,1:T(8,128)}), f32[384,256]{0,1:T(8,128)}) %reduce-scatter.19.cloned.1.call-update) | async-done | bytes 393232 | tf_op jit(solution)/shard_map/reduce_scatter | solution.py:245
  552.5 10.4 %reduce-scatter.21.cloned.1.call-done = bf16[96,1024]{1,0:T(8,128)(2,1)} async-done(((bf16[384,1024]{1,0:T(8,128)(2,1)}), bf16[96,1024]{1,0:T(8,128)(2,1)}) %reduce-scatter.21.cloned.1.call-update) | async-done | bytes 196624 | tf_op jit(solution)/shard_map/reduce_scatter | solution.py:266
  565.4 38.8 %all-reduce = (f32[1024]{0:T(1024)}, f32[1024]{0:T(1024)}) all-reduce(f32[1024]{0:T(1024)S(1)} %get-tuple-element.324, f32[1024]{0:T(1024)S(1)} %copy-done.30), channel_id=1, replica_groups=mesh['shard'=8,'tensor'=4] {'shard','tensor'}, use_global_device_ids=true, to_apply=%region_27.28 | all-reduce | flops 2048 | bytes 16384 | tf_op jit(solution)/shard_map/psum | solution.py:282
  606.0 44.8 %reduce-scatter.29.cloned.1.call-done = f32[128,656]{0,1:T(8,128)} async-done(((f32[1024,656]{0,1:T(8,128)}), f32[128,656]{0,1:T(8,128)}) %reduce-scatter.29.cloned.1.call-update) | async-done | bytes 335888 | tf_op jit(solution)/shard_map/reduce_scatter | solution.py:280
  650.8 61.1 %reduce-scatter.27.cloned.1.call-done = f32[128,2,656]{0,2,1:T(8,128)} async-done(((f32[1024,2,656]{0,2,1:T(8,128)}), f32[128,2,656]{0,2,1:T(8,128)}) %reduce-scatter.27.cloned.1.call-update) | async-done | bytes 671760 | tf_op jit(solution)/shard_map/reduce_scatter | solution.py:279
  711.9 50.1 %reduce-scatter.23.cloned.1.call-done = f32[128,3,256]{2,0,1:T(8,128)} async-done(((f32[1024,3,256]{2,0,1:T(8,128)}), f32[128,3,256]{2,0,1:T(8,128)}) %reduce-scatter.23.cloned.1.call-update) | async-done | bytes 393232 | tf_op jit(solution)/shard_map/reduce_scatter | solution.py:277
  (245 shorter events, 150.2 us)
Async XLA Ops:
  7.2 31.9 %all-gather.6.cloned.1.call-start = ((), (), s32[]{:S(2)}) async-start(), calls=%async_computation.10 | async-start | bytes 1769472 | tf_op jit(solution)/shard_map/all_gather | solution.py:104
  9.0 60.0 %all-gather.8.cloned.1.call-start = ((), (), s32[]{:S(2)}) async-start(), calls=%async_computation.11 | async-start | bytes 1769472 | tf_op jit(solution)/shard_map/all_gather | solution.py:126
  42.0 55.2 %all-gather.10.cloned.1.call-start = ((), (), s32[]{:S(2)}) async-start(), calls=%async_computation.12 | async-start | bytes 1769472 | tf_op jit(solution)/shard_map/all_gather | solution.py:125
  44.6 109.9 %reduce-scatter.11.cloned.1.call-start = ((), (), s32[]{:S(2)}) async-start(), calls=%async_computation.13 | async-start | bytes 983040 | tf_op jit(solution)/shard_map/reduce_scatter | solution.py:172
  122.1 65.7 %all-gather.12.cloned.1.call-start = ((), (), s32[]{:S(2)}) async-start(), calls=%async_computation.14 | async-start | bytes 3022848 | tf_op jit(solution)/shard_map/all_gather | solution.py:106
  122.7 91.7 %all-gather.14.cloned.1.call-start = ((), (), s32[]{:S(2)}) async-start(), calls=%async_computation.15 | async-start | bytes 1511424 | tf_op jit(solution)/shard_map/all_gather | solution.py:107
  123.3 124.3 %reduce-scatter.15.cloned.1.call-start = ((), (), s32[]{:S(2)}) async-start(), calls=%async_computation.17 | async-start | bytes 983040 | tf_op jit(solution)/shard_map/reduce_scatter | solution.py:206
  153.0 61.4 %copy-start.12 = (bf16[384,1024]{1,0:T(8,128)(2,1)}, bf16[384,1024]{1,0:T(8,128)(2,1)S(1)}, u32[]{:S(2)}) copy-start(bf16[384,1024]{1,0:T(8,128)(2,1)S(1)} %all_gather.38) | copy-start | bytes 2359300
  224.1 48.4 %reduce-scatter.13.cloned.1.call-start = ((), (), s32[]{:S(2)}) async-start(), calls=%async_computation.16 | async-start | bytes 983040 | tf_op jit(solution)/shard_map/reduce_scatter | solution.py:188
  227.2 258.0 %reduce-scatter.17.cloned.1.call-start = ((), (), s32[]{:S(2)}) async-start(), calls=%async_computation.18 | async-start | bytes 3538944 | tf_op jit(solution)/shard_map/reduce_scatter | solution.py:242
  439.6 95.5 %reduce-scatter.19.cloned.1.call-start = ((), (), s32[]{:S(2)}) async-start(), calls=%async_computation.19 | async-start | bytes 3538944 | tf_op jit(solution)/shard_map/reduce_scatter | solution.py:245
  443.6 42.6 %copy-start.26 = (f32[384,32]{0,1:T(8,128)S(1)}, f32[384,32]{0,1:T(8,128)}, u32[]{:S(2)}) copy-start(f32[384,32]{0,1:T(8,128)} %copy-done.25) | copy-start | bytes 147460
  443.6 42.6 %copy-start.27 = (f32[384,32]{0,1:T(8,128)S(1)}, f32[384,32]{0,1:T(8,128)}, u32[]{:S(2)}) copy-start(f32[384,32]{0,1:T(8,128)} %get-tuple-element.411) | copy-start | bytes 147460
  443.6 119.2 %reduce-scatter.21.cloned.1.call-start = ((), (), s32[]{:S(2)}) async-start(), calls=%async_computation.20 | async-start | bytes 983040 | tf_op jit(solution)/shard_map/reduce_scatter | solution.py:266
  486.3 53.2 %copy-start.2 = (bf16[384,1024]{1,0:T(8,128)(2,1)S(1)}, bf16[384,1024]{1,0:T(8,128)(2,1)}, u32[]{:S(2)}) copy-start(bf16[384,1024]{1,0:T(8,128)(2,1)} %copy-done.1) | copy-start | bytes 2359300
  486.3 53.2 %copy-start.20 = (bf16[384,4,64]{0,2,1:T(8,128)(2,1)S(1)}, bf16[384,4,64]{0,2,1:T(8,128)(2,1)}, u32[]{:S(2)}) copy-start(bf16[384,4,64]{0,2,1:T(8,128)(2,1)} %copy-done.19) | copy-start | bytes 589828
  486.4 54.5 %copy-start.21 = (bf16[384,4,64]{0,2,1:T(8,128)(2,1)}, bf16[384,4,64]{0,2,1:T(8,128)(2,1)S(1)}, u32[]{:S(2)}) copy-start(bf16[384,4,64]{0,2,1:T(8,128)(2,1)S(1)} %get-tuple-element.418) | copy-start | bytes 589828
  539.4 66.6 %reduce-scatter.25.cloned.1.call-start = ((), (), s32[]{:S(2)}) async-start(), calls=%async_computation.22 | async-start | bytes 1179648 | tf_op jit(solution)/shard_map/reduce_scatter | solution.py:278
  541.0 109.8 %reduce-scatter.29.cloned.1.call-start = ((), (), s32[]{:S(2)}) async-start(), calls=%async_computation.24 | async-start | bytes 3022848 | tf_op jit(solution)/shard_map/reduce_scatter | solution.py:280
  543.5 168.4 %reduce-scatter.27.cloned.1.call-start = ((), (), s32[]{:S(2)}) async-start(), calls=%async_computation.23 | async-start | bytes 6045696 | tf_op jit(solution)/shard_map/reduce_scatter | solution.py:279
  547.6 214.4 %reduce-scatter.23.cloned.1.call-start = ((), (), s32[]{:S(2)}) async-start(), calls=%async_computation.21 | async-start | bytes 3538944 | tf_op jit(solution)/shard_map/reduce_scatter | solution.py:277
  552.4 51.7 %copy-start.7 = (f32[96,1024]{1,0:T(8,128)S(1)}, f32[96,1024]{1,0:T(8,128)}, u32[]{:S(2)}) copy-start(f32[96,1024]{1,0:T(8,128)} %copy-done.6) | copy-start | bytes 1179652
  552.4 51.7 %copy-start.18 = (bf16[96,1024]{1,0:T(8,128)(2,1)S(1)}, bf16[96,1024]{1,0:T(8,128)(2,1)}, u32[]{:S(2)}) copy-start(bf16[96,1024]{1,0:T(8,128)(2,1)} %param.23) | copy-start | bytes 589828
  552.4 51.7 %copy-start.41 = (f32[96]{0:T(128)S(1)}, f32[96]{0:T(128)}, u32[]{:S(2)}) copy-start(f32[96]{0:T(128)} %copy-done.40) | copy-start | bytes 1156
  (40 other events, 443.2 us)
Sparse Core Ops, SparseCore 0:
  10.5 28.5 all-gather.5
  42.1 26.8 all-gather.7
  71.4 25.6 all-gather.9
  122.2 32.1 reduce-scatter.10
  156.2 31.5 all-gather.11
  189.5 24.8 all-gather.13
  224.2 23.3 reduce-scatter.14
  249.9 22.4 reduce-scatter.12
  439.7 45.4 reduce-scatter.16
  488.8 46.2 reduce-scatter.18
  539.5 23.2 reduce-scatter.20
  566.4 35.3 reduce-scatter.24
  605.8 44.9 reduce-scatter.28
  654.6 57.1 reduce-scatter.26
  715.7 46.2 reduce-scatter.22
where the time goes:
time: 779 us; the launch traced here: 769 us
  waiting for transfers between devices  376 us (48%)
  local copies, waits for them, and re-layouts  142 us (18%)
  blocking collectives  139 us (18%)
  matrix products  67.6 us (9%)
  other arithmetic  26.5 us (3%)
  between operations  14.9 us (2%)
    dynamic_update_slice x8, local copies, waits for them, and re-layouts, on_device(): lax.scan(joint_pass, zeros_heads, key_stack)  111 us
    reduce_scatter x1, waiting for transfers between devices, on_device(): lax.psum_scatter(in_grad, 'shard', scatter_dimension=0, tiled=True)  61.1 us
    reduce_scatter x1, waiting for transfers between devices, on_device(): lax.psum_scatter(qkv_grad_w, 'shard', scatter_dimension=0, tiled=True)  50.1 us
    reduce_scatter x1, waiting for transfers between devices, on_device(): lax.psum_scatter(value_parts.reshape(all_rows, local_width), 'shard', sca...  48.6 us
    reduce_scatter x1, waiting for transfers between devices, on_device(): lax.psum_scatter(down_grad, 'shard', scatter_dimension=0, tiled=True)  44.8 us
    reduce_scatter x1, waiting for transfers between devices, on_device(): lax.psum_scatter(key_parts.reshape(all_rows, local_width), 'shard', scatt...  40.4 us
    psum x1, blocking collectives, on_device(): lax.psum((gain_one_grad, gain_two_grad), ('shard', 'tensor'))  38.8 us
    all_gather x1, blocking collectives, on_device(): cot_full = lax.all_gather(cotangent, 'tensor', axis=0, tiled=True)  29.6 us
  transfers between devices with their start and end apart: 15, of which 14 were waited for; matrix products, arithmetic and copies ran while one was open for 6% of the time, Pallas kernels for 0%

commit v1 on v0

v1 whole, which is shorter than its diff:
```python
import jax
import jax.numpy as jnp
from jax import lax
from jax.experimental import pallas as pl
from jax.experimental.pallas import tpu as pltpu
from jax.sharding import PartitionSpec as P

HEAD_DIM = 64
EPSILON = 1e-05
THETA = 160000.0
MASKED = -1e30
MESH = pl.DeviceIdType.MESH
VMEM_BYTES = 56 * 1024 * 1024
FWD_CHUNK = 512
BWD_CHUNK = 256


def norm_rows(values, gain):
    centred = values - jnp.mean(values, axis=-1, keepdims=True)
    variance = jnp.mean(centred * centred, axis=-1, keepdims=True)
    return centred * lax.rsqrt(variance + EPSILON) * gain


def doc_layout(index, doc_starts):
    begun = doc_starts[None, :] <= index[:, None]
    segment = jnp.sum(begun.astype(jnp.int32), axis=1) - 1
    opening = jnp.max(jnp.where(begun, doc_starts[None, :], 0), axis=1)
    return (segment, index - opening)


def turning(position, head_width):
    halfway = head_width // 2
    inverse = THETA ** (-jnp.arange(halfway, dtype=jnp.float32) * 2.0 / head_width)
    angles = position.astype(jnp.float32)[:, None] * inverse[None, :]
    return (jnp.cos(angles)[:, None, :], jnp.sin(angles)[:, None, :])


def rotate(values, cosine, sine, direction):
    halfway = values.shape[-1] // 2
    leading = values[..., :halfway]
    trailing = values[..., halfway:]
    return jnp.concatenate(
        [
            leading * cosine - direction * trailing * sine,
            trailing * cosine + direction * leading * sine,
        ],
        axis=-1,
    )


def geglu(gate, upward):
    return jax.nn.gelu(gate, approximate=False) * upward


class Transfers:
    def __init__(self, items):
        self.items = items
        self.sizes = [lax.axis_size(axis) for _, axis, _ in items]

    def shapes(self):
        shapes = []
        for (value, _, kind), size in zip(self.items, self.sizes):
            if kind in ("gather", "spread"):
                shape = (size,) + value.shape
            else:
                shape = value.shape
            shapes.append(jax.ShapeDtypeStruct(shape, value.dtype))
        return shapes

    def scratch(self):
        semaphores = []
        for size in self.sizes:
            semaphores += [pltpu.SemaphoreType.DMA((2 * size,)), pltpu.SemaphoreType.DMA((2 * size,))]
        return semaphores + [pltpu.SemaphoreType.DMA((len(self.items),))]

    def barrier(self):
        barrier = pltpu.get_barrier_semaphore()
        total = 0
        for axis in ("shard", "tensor"):
            if any(other == axis for _, other, _ in self.items):
                size = lax.axis_size(axis)
                me = lax.axis_index(axis)
                for step in range(1, size):
                    pl.semaphore_signal(
                        barrier,
                        inc=1,
                        device_id={axis: lax.rem(me + step, size)},
                        device_id_type=MESH,
                    )
                total += size - 1
        pl.semaphore_wait(barrier, total)

    def start(self, in_refs, out_refs, sems):
        self.barrier()
        local_sem = sems[-1]
        self.sent, self.landing, self.passing = [], [], []
        for place, (_, axis, kind) in enumerate(self.items):
            source, target = in_refs[place], out_refs[place]
            send, recv = sems[2 * place], sems[2 * place + 1]
            size = self.sizes[place]
            me = lax.axis_index(axis)

            def post(src, dst, slot, peer, axis=axis, send=send, recv=recv):
                copy = pltpu.make_async_remote_copy(
                    src_ref=src,
                    dst_ref=dst,
                    send_sem=send.at[slot],
                    recv_sem=recv.at[slot],
                    device_id={axis: peer},
                    device_id_type=MESH,
                )
                return copy

            if kind == "gather" or kind == "swap":
                for step in range(1, size):
                    peer, origin = lax.rem(me + step, size), lax.rem(me + size - step, size)
                    src = source if kind == "gather" else source.at[peer]
                    copy = post(src, target.at[me], step, peer)
                    copy.start()
                    self.sent.append(copy)
                    self.landing.append(post(src, target.at[origin], step, peer))
                own = source if kind == "gather" else source.at[me]
                keep = pltpu.make_async_copy(own, target.at[me], local_sem.at[place])
                keep.start()
                self.sent.append(keep)
            else:
                chips = size // 2
                chip, core = lax.div(me, 2), lax.rem(me, 2)
                partner = me + 1 - 2 * core
                if kind == "pair":
                    copy = post(source.at[1 - core], target.at[1 - core], 0, partner)
                    copy.start()
                    self.sent.append(copy)
                    self.landing.append(post(source.at[core], target.at[core], 0, partner))
                    keep = pltpu.make_async_copy(
                        source.at[core], target.at[1 - core], local_sem.at[place]
                    )
                    keep.start()
                    self.sent.append(keep)
                    continue
                for step in range(1, chips):
                    far, origin = lax.rem(chip + step, chips), lax.rem(chip + chips - step, chips)
                    peer = 2 * far + core
                    if kind == "spread":
                        copy = post(source, target.at[me], step, peer)
                        block = target.at[2 * origin + core]
                        other = target.at[2 * origin + 1 - core]
                        arrive = post(source, block, step, peer)
                        onward = post(block, block, size + step, partner)
                        self.passing.append(
                            (arrive, onward, post(block, other, size + step, partner))
                        )
                    else:
                        copy = post(source.at[far], target.at[chip], step, peer)
                        self.landing.append(
                            post(source.at[far], target.at[origin], step, peer)
                        )
                    copy.start()
                    self.sent.append(copy)
                if kind == "spread":
                    copy = post(source, target.at[me], 0, partner)
                    copy.start()
                    self.sent.append(copy)
                    self.landing.append(post(source, target.at[partner], 0, partner))
                    keep = pltpu.make_async_copy(source, target.at[me], local_sem.at[place])
                else:
                    keep = pltpu.make_async_copy(
                        source.at[chip], target.at[chip], local_sem.at[place]
                    )
                keep.start()
                self.sent.append(keep)

    def finish(self):
        for arrive, onward, _ in self.passing:
            arrive.wait_recv()
            onward.start()
        for _, onward, other in self.passing:
            onward.wait_send()
            other.wait_recv()
        for copy in self.landing:
            copy.wait_recv()
        for copy in self.sent:
            if hasattr(copy, "wait_send") and copy.is_remote:
                copy.wait_send()
            else:
                copy.wait()


ANY = pl.BlockSpec(memory_space=pl.ANY)
WHOLE = pl.BlockSpec(memory_space=pltpu.VMEM)


def run_kernel(ident, name, moves, work=None, arrays=(), results=(), scratch=(), cost=None):
    transfers = Transfers(moves)
    carried, count = len(moves), len(arrays)

    def kernel(*refs):
        refs = list(refs)
        array_refs, in_refs = refs[:count], refs[count : count + carried]
        refs = refs[count + carried :]
        result_refs, out_refs = refs[: len(results)], refs[len(results) : len(results) + carried]
        refs = refs[len(results) + carried :]
        scratch_refs, sems = refs[: len(scratch)], refs[len(scratch) :]
        transfers.start(in_refs, out_refs, sems)
        if work is not None:
            work(*array_refs, *result_refs, *scratch_refs)
        transfers.finish()

    return pl.pallas_call(
        kernel,
        out_shape=tuple(results) + tuple(transfers.shapes()),
        in_specs=[WHOLE] * count + [ANY] * carried,
        out_specs=tuple([WHOLE] * len(results) + [ANY] * carried),
        scratch_shapes=list(scratch) + transfers.scratch(),
        compiler_params=pltpu.CompilerParams(
            collective_id=ident,
            has_side_effects=True,
            vmem_limit_bytes=VMEM_BYTES if work is not None else None,
        ),
        cost_estimate=cost,
        name=name,
    )(*arrays, *[value for value, _, _ in moves])


def attend_forward(
    keys_values, turned_pairs, turned_query, key_segment, query_segment, out, log_total, held
):
    total = keys_values.shape[0]
    wide = turned_query.shape[1]
    held[...] = jnp.zeros_like(held)
    query = turned_query[...]
    mine = query_segment[...]

    def step(index, carry):
        highest, summed = carry
        rows = pl.ds(pl.multiple_of(index * FWD_CHUNK, FWD_CHUNK), FWD_CHUNK)
        scores = jnp.dot(keys_values[rows, :], query, preferred_element_type=jnp.float32)
        scores = jnp.where(key_segment[rows, :] == mine, scores, MASKED)
        raised = jnp.maximum(highest, jnp.max(scores, axis=0, keepdims=True))
        lowered = jnp.exp(highest - raised)
        weights = jnp.exp(scores - raised)
        summed = summed * lowered + jnp.sum(weights, axis=0, keepdims=True)
        held[...] = held[...] * lowered + jnp.dot(
            turned_pairs[HEAD_DIM:, rows],
            weights.astype(jnp.bfloat16),
            preferred_element_type=jnp.float32,
        )
        return (raised, summed)

    highest, summed = lax.fori_loop(
        0,
        total // FWD_CHUNK,
        step,
        (jnp.full((1, wide), MASKED, jnp.float32), jnp.zeros((1, wide), jnp.float32)),
    )
    out[...] = held[...] / summed
    log_total[...] = highest + jnp.log(summed)


def attend_backward(
    keys_values,
    turned_pairs,
    turned_query,
    turned_grad,
    query_wide,
    grad_wide,
    key_segment,
    query_segment,
    log_total,
    attended,
    pair_grad,
    query_grad,
):
    total = keys_values.shape[0]
    query_grad[...] = jnp.zeros_like(query_grad)
    query = turned_query[...]
    grad = turned_grad[...]
    mine = query_segment[...]
    logs = log_total[...]
    delta = jnp.sum(grad[HEAD_DIM:, :].astype(jnp.float32) * attended[...], axis=0, keepdims=True)

    def step(index, carry):
        rows = pl.ds(pl.multiple_of(index * BWD_CHUNK, BWD_CHUNK), BWD_CHUNK)
        pairs = keys_values[rows, :]
        scores = jnp.dot(pairs, query, preferred_element_type=jnp.float32)
        weights = jnp.exp(
            jnp.where(key_segment[rows, :] == mine, scores - logs, MASKED)
        )
        weight_grad = jnp.dot(pairs, grad, preferred_element_type=jnp.float32)
        score_grad = (weights * (weight_grad - delta)).astype(jnp.bfloat16)
        pair_grad[rows, :] = (
            jnp.dot(score_grad, query_wide[...], preferred_element_type=jnp.float32)
            + jnp.dot(
                weights.astype(jnp.bfloat16), grad_wide[...], preferred_element_type=jnp.float32
            )
        ).astype(pair_grad.dtype)
        query_grad[...] += jnp.dot(
            turned_pairs[:HEAD_DIM, rows], score_grad, preferred_element_type=jnp.float32
        )
        return carry

    lax.fori_loop(0, total // BWD_CHUNK, step, 0)


def fold_rows(values, padded):
    half = values.shape[-2] // 2
    folded = jnp.concatenate([values[..., :half, :], values[..., half:, :]], axis=-1)
    extra = padded - half
    if extra:
        folded = jnp.pad(folded, [(0, 0)] * (folded.ndim - 2) + [(0, extra), (0, 0)])
    return folded


def unfold_rows(folded, half):
    folded = folded[..., :half, :]
    return jnp.concatenate([folded[..., :HEAD_DIM], folded[..., HEAD_DIM:]], axis=-2)


def on_device(
    tokens,
    doc_starts,
    norm1_gain,
    qkv_weight,
    out_weight,
    norm2_gain,
    in_weight,
    down_weight,
    cotangent,
):
    row_count, model_width = tokens.shape
    local_width = qkv_weight.shape[2]
    unit_width = in_weight.shape[2]
    head_dim = HEAD_DIM
    heads = local_width // head_dim
    shards = lax.axis_size("shard")
    tensors = lax.axis_size("tensor")
    me_shard = lax.axis_index("shard")
    group_rows = row_count * tensors
    all_rows = group_rows * shards
    parts = shards // heads
    part_rows = group_rows // parts
    half = part_rows // 2
    padded = -(-half // 16) * 16
    query_rows = shards * part_rows
    group_index = me_shard * group_rows + jnp.arange(group_rows, dtype=jnp.int32)
    segment, position = doc_layout(group_index, doc_starts)
    cosine, sine = turning(position, head_dim)
    contract_rows = (((0,), (0,)), ((), ()))
    contract_cols = (((1,), (1,)), ((), ()))
    shape_heads = (group_rows, heads, head_dim)
    bf16, f32 = jnp.bfloat16, jnp.float32

    def to_parts(values):
        return (
            values.reshape(parts, part_rows, heads, head_dim)
            .transpose(2, 0, 1, 3)
            .reshape(shards, part_rows, head_dim)
        )

    def from_parts(values):
        return (
            values.reshape(heads, parts, part_rows, head_dim)
            .transpose(1, 2, 0, 3)
            .reshape(group_rows, local_width)
        )

    resid_in = tokens.astype(f32)
    normed_one, norm_one_back = jax.vjp(norm_rows, resid_in, norm1_gain)
    rows_one, qkv_full = run_kernel(
        1,
        "gather_inputs",
        [
            (normed_one.astype(bf16), "tensor", "gather"),
            (qkv_weight.reshape(-1, 3 * local_width), "shard", "spread"),
        ],
    )
    rows_one = rows_one.reshape(group_rows, model_width)
    qkv_mat = qkv_full.reshape(model_width, 3 * local_width)
    projected = jnp.dot(rows_one, qkv_mat, preferred_element_type=f32)
    score_scale = head_dim ** (-0.5)
    query = rotate(projected[:, :local_width].reshape(shape_heads), cosine, sine, 1.0).astype(bf16)
    keys = rotate(
        projected[:, local_width : 2 * local_width].reshape(shape_heads), cosine, sine, 1.0
    ).astype(bf16)
    values = projected[:, 2 * local_width :].astype(bf16).reshape(shape_heads)
    pairs = jnp.concatenate([keys, values], axis=-1).transpose(1, 0, 2)
    pairs = jnp.broadcast_to(pairs[:, None], (heads, parts, group_rows, 2 * head_dim)).reshape(
        shards, group_rows, 2 * head_dim
    )
    folded_query = fold_rows(to_parts(query * jnp.asarray(score_scale, bf16)), padded)
    sent_qkv, out_full = run_kernel(
        2,
        "swap_heads",
        [
            (jnp.concatenate([pairs, folded_query], axis=1), "shard", "swap"),
            (out_weight, "shard", "spread"),
        ],
    )
    out_full = out_full.reshape(model_width, local_width)
    keys_values = sent_qkv[:, :group_rows].reshape(all_rows, 2 * head_dim)
    turned_pairs = keys_values.T
    query_mine = unfold_rows(sent_qkv[:, group_rows:], half).reshape(query_rows, head_dim)
    no_query = jnp.zeros_like(query_mine)
    query_wide = jnp.concatenate([query_mine, no_query], axis=1)
    turned_query = query_wide.T
    key_segment, _ = doc_layout(jnp.arange(all_rows, dtype=jnp.int32), doc_starts)
    mine = lax.rem(me_shard, parts) * part_rows
    query_segment = lax.dynamic_slice_in_dim(
        key_segment.reshape(shards, group_rows), mine, part_rows, axis=1
    ).reshape(1, query_rows)
    key_segment = key_segment.reshape(all_rows, 1)
    attended_turned, log_total, in_full, cot_full = run_kernel(
        3,
        "attend_forward",
        [
            (in_weight.reshape(-1, 2 * unit_width), "shard", "spread"),
            (cotangent, "tensor", "gather"),
        ],
        attend_forward,
        (keys_values, turned_pairs, turned_query, key_segment, query_segment),
        (
            jax.ShapeDtypeStruct((head_dim, query_rows), f32),
            jax.ShapeDtypeStruct((1, query_rows), f32),
        ),
        (pltpu.VMEM((head_dim, query_rows), f32),),
    )
    in_mat = in_full.reshape(model_width, 2 * unit_width)
    cot_full = cot_full.reshape(group_rows, model_width)
    attended_back = fold_rows(
        attended_turned.astype(bf16).T.reshape(shards, part_rows, head_dim), padded
    )
    (attended_parts,) = run_kernel(4, "return_heads", [(attended_back, "shard", "swap")])
    attended = from_parts(unfold_rows(attended_parts, half))

    def share(left, right):
        return (
            lax.dot_general(left, right, contract_cols, preferred_element_type=f32)
            .astype(bf16)
            .reshape(tensors, row_count, model_width)
        )

    out_parts, down_full = run_kernel(
        5,
        "out_shares",
        [(share(attended, out_full), "tensor", "swap"), (down_weight, "shard", "spread")],
    )
    down_full = down_full.reshape(model_width, unit_width)
    resid_mid = resid_in + jnp.sum(out_parts.astype(f32), axis=0)
    normed_two, norm_two_back = jax.vjp(norm_rows, resid_mid, norm2_gain)
    (rows_two,) = run_kernel(6, "gather_middle", [(normed_two.astype(bf16), "tensor", "gather")])
    rows_two = rows_two.reshape(group_rows, model_width)
    gate_up = jnp.dot(rows_two, in_mat, preferred_element_type=f32)
    active, geglu_back = jax.vjp(geglu, gate_up[:, :unit_width], gate_up[:, unit_width:])
    active = active.astype(bf16)
    active_grad = jnp.dot(cot_full, down_full, preferred_element_type=f32)
    gate_grad, up_grad = geglu_back(active_grad)
    gate_up_grad = jnp.concatenate([gate_grad, up_grad], axis=1).astype(bf16)
    in_grad = lax.dot_general(rows_two, gate_up_grad, contract_rows, preferred_element_type=f32)
    down_grad = lax.dot_general(cot_full, active, contract_rows, preferred_element_type=f32)

    def by_core(grad):
        return (
            grad.astype(bf16)
            .reshape(shards // 2, 2, model_width // shards, grad.shape[1])
            .transpose(1, 0, 2, 3)
        )

    two_parts, in_pair, down_pair = run_kernel(
        7,
        "middle_grad_shares",
        [
            (share(gate_up_grad, in_mat), "tensor", "swap"),
            (by_core(in_grad), "shard", "pair"),
            (by_core(down_grad), "shard", "pair"),
        ],
    )
    normed_two_grad = jnp.sum(two_parts.astype(f32), axis=0)
    mid_part, gain_two_grad = norm_two_back(normed_two_grad)
    mid_grad = cotangent.astype(f32) + mid_part
    (branch_full,) = run_kernel(
        8, "gather_branch", [(mid_grad.astype(bf16), "tensor", "gather")]
    )
    branch_full = branch_full.reshape(group_rows, model_width)
    out_grad = lax.dot_general(branch_full, attended, contract_rows, preferred_element_type=f32)
    attended_grad = jnp.dot(branch_full, out_full, preferred_element_type=f32).astype(bf16)
    (grad_parts,) = run_kernel(
        9,
        "swap_grads",
        [(fold_rows(to_parts(attended_grad.reshape(shape_heads)), padded), "shard", "swap")],
    )
    grad_mine = unfold_rows(grad_parts, half).reshape(query_rows, head_dim)
    grad_wide = jnp.concatenate([jnp.zeros_like(grad_mine), grad_mine], axis=1)

    def add_pair(pair):
        return jnp.sum(pair.astype(f32), axis=0).astype(bf16)

    by_shard = (shards, model_width // shards)
    pair_grad, query_grad_turned, mixed_parts, in_parts, down_parts, out_grads = run_kernel(
        10,
        "attend_backward",
        [
            (share(active, down_full), "tensor", "swap"),
            (add_pair(in_pair), "shard", "mates"),
            (add_pair(down_pair), "shard", "mates"),
            (out_grad.astype(bf16).reshape(*by_shard, local_width), "shard", "swap"),
        ],
        attend_backward,
        (
            keys_values,
            turned_pairs,
            turned_query,
            grad_wide.T,
            query_wide,
            grad_wide,
            key_segment,
            query_segment,
            log_total,
            attended_turned,
        ),
        (
            jax.ShapeDtypeStruct((all_rows, 2 * head_dim), bf16),
            jax.ShapeDtypeStruct((head_dim, query_rows), f32),
        ),
    )
    mixed = (resid_mid + jnp.sum(mixed_parts.astype(f32), axis=0)).astype(bf16)
    folded_grad = fold_rows(
        query_grad_turned.astype(bf16).T.reshape(shards, part_rows, head_dim), padded
    )
    (qkv_back,) = run_kernel(
        11,
        "return_grads",
        [
            (
                jnp.concatenate(
                    [pair_grad.reshape(shards, group_rows, 2 * head_dim), folded_grad], axis=1
                ),
                "shard",
                "swap",
            )
        ],
    )
    query_rot_grad = from_parts(unfold_rows(qkv_back[:, group_rows:], half)).reshape(shape_heads)
    pair_sum = jnp.sum(
        qkv_back[:, :group_rows].reshape(heads, parts, group_rows, 2 * head_dim).astype(f32), axis=1
    ).transpose(1, 0, 2)
    query_grad = rotate(query_rot_grad.astype(f32) * score_scale, cosine, sine, -1.0).astype(bf16)
    key_grad = rotate(pair_sum[..., :head_dim], cosine, sine, -1.0).astype(bf16)
    qkv_grad = jnp.concatenate(
        [
            query_grad.reshape(group_rows, local_width),
            key_grad.reshape(group_rows, local_width),
            pair_sum[..., head_dim:].astype(bf16).reshape(group_rows, local_width),
        ],
        axis=1,
    )
    qkv_grad_w = lax.dot_general(rows_one, qkv_grad, contract_rows, preferred_element_type=f32)
    one_share = lax.dot_general(qkv_grad, qkv_mat, contract_cols, preferred_element_type=f32)
    gain_one_share = jnp.sum(one_share * rows_one.astype(f32), axis=0) / norm1_gain
    gains = jnp.concatenate([gain_one_share, gain_two_grad]).reshape(-1, 128)
    one_parts, qkv_parts, gain_parts = run_kernel(
        12,
        "input_grad_shares",
        [
            (one_share.astype(bf16).reshape(tensors, row_count, model_width), "tensor", "swap"),
            (qkv_grad_w.astype(bf16).reshape(*by_shard, 3 * local_width), "shard", "swap"),
            (gains, "shard", "gather"),
        ],
    )
    (gain_all,) = run_kernel(
        13, "gather_gains", [(jnp.sum(gain_parts, axis=0), "tensor", "gather")]
    )
    gain_all = jnp.sum(gain_all, axis=0).reshape(2, model_width)
    normed_one_grad = jnp.sum(one_parts.astype(f32), axis=0)
    input_part, _ = norm_one_back(normed_one_grad)
    tokens_grad = (mid_grad + input_part).astype(bf16)

    def add_up(pieces, shape):
        return jnp.sum(pieces.astype(f32), axis=0).reshape(shape)

    return (
        mixed,
        tokens_grad,
        gain_all[0],
        add_up(qkv_parts, qkv_weight.shape),
        add_up(out_grads, out_weight.shape),
        gain_all[1],
        add_up(in_parts, in_weight.shape),
        add_up(down_parts, down_weight.shape),
    )


def solution(mesh):
    in_specs = (
        P(("shard", "tensor"), None),
        P(),
        P(),
        P("shard", None, "tensor"),
        P("shard", "tensor"),
        P(),
        P("shard", None, "tensor"),
        P("shard", "tensor"),
        P(("shard", "tensor"), None),
    )
    out_specs = (
        P(("shard", "tensor"), None),
        P(("shard", "tensor"), None),
        P(),
        P("shard", None, "tensor"),
        P("shard", "tensor"),
        P(),
        P("shard", None, "tensor"),
        P("shard", "tensor"),
    )
    return jax.shard_map(
        on_device, mesh=mesh, in_specs=in_specs, out_specs=out_specs, check_vma=False
    )
```

time: 779 us -> 417 us (0.54); the launches traced: 769 us -> 416 us
  waiting for transfers between devices: 376 us -> 0 us
  Pallas kernels: 0 us -> 301 us
  blocking collectives: 139 us -> 0 us
  local copies, waits for them, and re-layouts: 142 us -> 46.3 us
  matrix products: 67.6 us -> 26.2 us
  other arithmetic: 26.5 us -> 40.7 us
  between operations: 14.9 us -> 1.57 us
    pallas_call x0 -> x13, Pallas kernels: none -> 301 us  [run_kernel(): pl.pallas_call(kernel, out_shape=tuple(results) + tuple(transfers.shapes(...]
    reduce_scatter x10 -> x0, waiting for transfers between devices: 300 us -> none  [the longest x1 61.1 us: on_device(): lax.psum_scatter(in_grad, 'shard', scatter_dimension=0, tiled=True)]
    dynamic_update_slice x8 -> x0, local copies, waits for them, and re-layouts: 111 us -> none  [on_device(): lax.scan(joint_pass, zeros_heads, key_stack)]
    all_gather x5 -> x0, blocking collectives: 101 us -> none  [the longest x1 29.6 us: on_device(): cot_full = lax.all_gather(cotangent, 'tensor', axis=0, tiled=True)]
    all_gather x5 -> x0, waiting for transfers between devices: 74.9 us -> none  [the longest x1 25.6 us: on_device(): lax.all_gather(keys_flat, 'shard', axis=0, tiled=True)]
    dot_general x23 -> x9, matrix products: 59.9 us -> 18.7 us  [the longest x3 5.48 us: share(): lax.dot_general(left, right, contract_cols, preferred_element_type=f32)]
    psum x1 -> x0, blocking collectives: 38.8 us -> none  [on_device(): lax.psum((gain_one_grad, gain_two_grad), ('shard', 'tensor'))]
    reshape x1 -> x10, local copies, waits for them, and re-layouts: 2.41 us -> 20.4 us  [the longest x4 16.4 us: by_core(): return grad.astype(bf16).reshape(shards // 2, 2, model_width // shards, g...]
  transfers between devices with their start and end apart: 15 -> 0, of which waited for: 14 -> 0; matrix products, arithmetic and copies ran while one was open for 6% -> 0% of each run, Pallas kernels for 0% -> 0%
where the time goes in v1:
time: 417 us; the launch traced here: 416 us
  Pallas kernels  301 us (72%)
  local copies, waits for them, and re-layouts  46.3 us (11%)
  other arithmetic  40.7 us (10%)
  matrix products  26.2 us (6%)
    pallas_call x13, Pallas kernels, run_kernel(): pl.pallas_call(kernel, out_shape=tuple(results) + tuple(transfers.shapes(...  301 us
    reshape x4, local copies, waits for them, and re-layouts, by_core(): return grad.astype(bf16).reshape(shards // 2, 2, model_width // shards, g...  16.4 us

profile of v1, /device:TPU:0, one launch (start us, length us, event | category | flops | bytes accessed | tf_op | source)
XLA Modules:
  0.0 416.0 jit_solution(9185253397208391166)
XLA Ops:
  14.0 21.5 %gather_inputs.1 = (bf16[4,96,1024]{2,1,0:T(8,128)(2,1)}, bf16[8,128,768]{2,1,0:T(8,128)(2,1)}) custom-call(bf16[96,1024]{1,0:T(8,128)(2,1)} %fusion.13.refs_0_, bf16[128,768]{1,0:T(8,128)(2,1)} %copy.134.refs_1_), custom_call_target="tpu_custom_call" | custom-call | tf_op jit(solution)/shard_map/gather_inputs/pallas_call | solution.py:209
  35.4 2.4 fusion.42
  41.9 2.4 subtract_convert_fusion.3
  49.4 18.7 %swap_heads.1 = (bf16[8,480,128]{2,1,0:T(8,128)(2,1)}, bf16[8,128,256]{2,1,0:T(8,128)(2,1)}) custom-call(bf16[8,480,128]{2,1,0:T(8,128)(2,1)} %maximum_maximum_fusion.refs_0_, bf16[128,256]{1,0:T(8,128)(2,1)} %refs_1_.2), custom_call_target="tpu_custom_call" | custom-call | tf_op jit(solution)/shard_map/swap_heads/pallas_call | solution.py:209
  73.6 29.0 %attend_forward.1 = (f32[64,1536]{1,0:T(8,128)}, f32[1,1536]{1,0:T(1,128)}, bf16[8,128,1312]{2,1,0:T(8,128)(2,1)}, bf16[4,96,1024]{2,1,0:T(8,128)(2,1)}) custom-call(bf16[3072,128]{1,0:T(8,128)(2,1)} %bitcast.100, bf16[128,3072]{1,0:T(8,128)(2,1)} %bitcast.105, bf16[128,1536]{1,0:T(8,128)(2,1)} %copy.147.refs_2_, s32[3072,1]{1,0:T(8,128)} %copy.148.refs_3_.refs_6_, ...), custom_call_target="tpu_custom_call" | custom-call | tf_op jit(solution)/shard_map/attend_forward/pallas_call | solution.py:209
  104.7 5.9 %return_heads.1 = bf16[8,96,128]{2,1,0:T(8,128)(2,1)} custom-call(bf16[8,96,128]{2,1,0:T(8,128)(2,1)} %pad_maximum_fusion.11.refs_0_), custom_call_target="tpu_custom_call" | custom-call | tf_op jit(solution)/shard_map/return_heads/pallas_call | solution.py:209
  113.6 17.9 %out_shares.1 = (bf16[4,96,1024]{2,1,0:T(8,128)(2,1)}, bf16[8,128,656]{2,1,0:T(8,128)(2,1)}) custom-call(bf16[4,96,1024]{2,1,0:T(8,128)(2,1)} %bitcast.112, bf16[128,656]{1,0:T(8,128)(2,1)} %copy.152.refs_1_), custom_call_target="tpu_custom_call" | custom-call | tf_op jit(solution)/shard_map/out_shares/pallas_call | solution.py:209
  134.0 19.5 %gather_middle.1 = bf16[4,96,1024]{2,1,0:T(8,128)(2,1)} custom-call(bf16[96,1024]{1,0:T(8,128)(2,1)} %multiply_convert_fusion.2.refs_0_), custom_call_target="tpu_custom_call" | custom-call | tf_op jit(solution)/shard_map/gather_middle/pallas_call | solution.py:209
  153.5 3.7 fusion.43
  163.2 2.3 convolution_convert_fusion.4
  167.4 3.4 copy.154
  170.8 4.1 convolution_convert_fusion
  174.9 6.3 %reshape.308 = bf16[4,2,128,1312]{2,1,0,3:T(2,128)(2,1)S(1)} reshape(bf16[1024,1312]{0,1:T(8,128)(2,1)} %convolution_convert_fusion) | data formatting | bytes 5373952 | tf_op jit(solution)/shard_map/reshape | solution.py:464
  181.2 5.8 %copy.153 = bf16[4,2,128,1312]{3,2,0,1:T(8,128)(2,1)} copy(bf16[4,2,128,1312]{2,1,0,3:T(2,128)(2,1)S(1)} %reshape.308) | data formatting | bytes 5373952 | tf_op jit(solution)/shard_map/reshape | solution.py:464
  187.0 81.3 %middle_grad_shares.1 = (bf16[4,96,1024]{2,1,0:T(8,128)(2,1)}, bf16[2,4,128,1312]{3,2,1,0:T(8,128)(2,1)}, bf16[2,4,128,656]{3,2,1,0:T(8,128)(2,1)}) custom-call(bf16[4,96,1024]{2,1,0:T(8,128)(2,1)} %bitcast.132, bf16[2,4,128,1312]{3,2,1,0:T(8,128)(2,1)} %bitcast.102, bf16[2,4,128,656]{3,2,1,0:T(8,128)(2,1)} %bitcast.110), custom_call_target="tpu_custom_call" | custom-call | tf_op jit(solution)/shard_map/middle_grad_shares/pallas_call | solution.py:209
  271.0 16.4 %gather_branch.1 = bf16[4,96,1024]{2,1,0:T(8,128)(2,1)} custom-call(bf16[96,1024]{1,0:T(8,128)(2,1)} %fusion.15.refs_0_), custom_call_target="tpu_custom_call" | custom-call | tf_op jit(solution)/shard_map/gather_branch/pallas_call | solution.py:209
  291.7 6.2 %swap_grads.1 = bf16[8,96,128]{2,1,0:T(8,128)(2,1)} custom-call(bf16[8,96,128]{2,1,0:T(8,128)(2,1)} %pad_maximum_fusion.12.refs_0_), custom_call_target="tpu_custom_call" | custom-call | tf_op jit(solution)/shard_map/swap_grads/pallas_call | solution.py:209
  301.1 2.8 reduce_sum.252.refs_12_
  303.9 3.9 reduce_sum.251.refs_11_
  307.8 42.2 %attend_backward.1 = (bf16[3072,128]{1,0:T(8,128)(2,1)}, f32[64,1536]{1,0:T(8,128)}, bf16[4,96,1024]{2,1,0:T(8,128)(2,1)}, bf16[4,128,1312]{2,1,0:T(8,128)(2,1)}...) custom-call(bf16[3072,128]{1,0:T(8,128)(2,1)} %bitcast.101, bf16[128,3072]{1,0:T(8,128)(2,1)} %bitcast.106, ...), custom_call_target="tpu_custom_call" | custom-call | tf_op jit(solution)/shard_map/attend_backward/pallas_call | solution.py:209
  354.3 13.2 %return_grads.1 = bf16[8,480,128]{2,1,0:T(8,128)(2,1)} custom-call(bf16[8,480,128]{2,1,0:T(8,128)(2,1)} %maximum_maximum_fusion.1.refs_0_), custom_call_target="tpu_custom_call" | custom-call | tf_op jit(solution)/shard_map/return_grads/pallas_call | solution.py:209
  371.5 3.4 multiply_reduce_fusion
  377.6 23.6 %input_grad_shares.1 = (bf16[4,96,1024]{2,1,0:T(8,128)(2,1)}, bf16[8,128,768]{2,1,0:T(8,128)(2,1)}, f32[8,16,128]{2,1,0:T(8,128)}) custom-call(bf16[4,96,1024]{2,1,0:T(8,128)(2,1)} %bitcast.140, bf16[8,128,768]{2,1,0:T(8,128)(2,1)} %bitcast.116, f32[16,128]{1,0:T(8,128)} %pad_maximum_fusion.13.refs_2_), custom_call_target="tpu_custom_call" | custom-call | tf_op jit(solution)/shard_map/input_grad_shares/pallas_call | solution.py:209
  404.6 5.9 %gather_gains.1 = f32[4,16,128]{2,1,0:T(8,128)} custom-call(f32[16,128]{1,0:T(8,128)} %reduce_sum.260.refs_0_), custom_call_target="tpu_custom_call" | custom-call | tf_op jit(solution)/shard_map/gather_gains/pallas_call | solution.py:209
  (177 shorter events, 72.7 us)
Async XLA Ops:
  0.6 8.3 %copy-start.20 = (bf16[128,656]{0,1:T(8,128)(2,1)S(1)}, bf16[128,656]{0,1:T(8,128)(2,1)}, u32[]{:S(2)}) copy-start(bf16[128,656]{0,1:T(8,128)(2,1)} %param.16) | copy-start | bytes 503812
  0.6 9.2 %copy-start.19 = (bf16[128,2,656]{0,2,1:T(8,128)(2,1)S(1)}, bf16[128,2,656]{0,2,1:T(8,128)(2,1)}, u32[]{:S(2)}) copy-start(bf16[128,2,656]{0,2,1:T(8,128)(2,1)} %param.15) | copy-start | bytes 1007620
  45.4 2.6 copy-start.9
  45.4 2.6 copy-start.10
  70.5 3.1 copy-start
  104.7 7.5 %copy-start.4 = (bf16[8,128,256]{2,1,0:T(8,128)(2,1)S(1)}, bf16[8,128,256]{2,1,0:T(8,128)(2,1)}, u32[]{:S(2)}) copy-start(bf16[8,128,256]{2,1,0:T(8,128)(2,1)} %get-tuple-element.34) | copy-start | bytes 1572868
  112.2 20.6 %copy-start.7 = (bf16[384,256]{0,1:T(8,128)(2,1)}, bf16[384,256]{0,1:T(8,128)(2,1)S(1)}, u32[]{:S(2)}) copy-start(bf16[384,256]{0,1:T(8,128)(2,1)S(1)} %reshape.300) | copy-start | bytes 589828
  112.2 20.6 %copy-start.1 = (bf16[96,1024]{1,0:T(8,128)(2,1)S(1)}, bf16[96,1024]{1,0:T(8,128)(2,1)}, u32[]{:S(2)}) copy-start(bf16[96,1024]{1,0:T(8,128)(2,1)} %param.9) | copy-start | bytes 589828
  113.6 19.6 %copy-start.23 = (f32[1024]{0:T(1024)S(1)}, f32[1024]{0:T(1024)}, u32[]{:S(2)}) copy-start(f32[1024]{0:T(1024)} %param.14) | copy-start | bytes 12292
  157.1 2.3 copy-start.15
  157.2 2.3 copy-start.25
  160.7 1.8 copy-start.27
  160.7 2.5 copy-start.24
  167.4 3.4 copy-start.16
  167.4 3.4 copy-start.28
  268.3 1.9 copy-start.6
  269.9 17.5 %copy-start.5 = (bf16[8,128,256]{2,1,0:T(8,128)(2,1)S(1)}, bf16[8,128,256]{2,1,0:T(8,128)(2,1)}, u32[]{:S(2)}) copy-start(bf16[8,128,256]{2,1,0:T(8,128)(2,1)} %get-tuple-element.34) | copy-start | bytes 1572868
  270.2 18.8 %copy-start.8 = (bf16[384,256]{0,1:T(8,128)(2,1)S(1)}, bf16[384,256]{0,1:T(8,128)(2,1)}, u32[]{:S(2)}) copy-start(bf16[384,256]{0,1:T(8,128)(2,1)} %copy-done.7) | copy-start | bytes 589828
  350.0 2.1 copy-start.17
  350.0 2.8 copy-start.18
  353.2 14.4 %copy-start.13 = (bf16[4,128,656]{2,1,0:T(8,128)(2,1)S(1)}, bf16[4,128,656]{2,1,0:T(8,128)(2,1)}, u32[]{:S(2)}) copy-start(bf16[4,128,656]{2,1,0:T(8,128)(2,1)} %get-tuple-element.51) | copy-start | bytes 2015236
  371.4 3.4 copy-start.21
  371.5 4.0 copy-start.26
  411.9 2.9 copy-start.11
  (6 other events, 8.7 us)
